TPU v7x, 32 devices: a whole 2x2x4 slice. The times are simulated.
32 devices in a mesh: ctx: 16 (over z, y, core), tp: 2 (over x).
Axes of the slice: x: 2, y: 2, z: 4, core: 2. Of those that a mesh axis runs over, the one named last changes fastest.
Arguments:
- q_new: bfloat16 [256, 2048], P(('ctx', 'tp')), may hold values from -128 to 128
- kv_new: bfloat16 [2, 256, 256], P(None, 'ctx', 'tp'), may hold values from -4 to 4
- kv_cache: bfloat16 [2, 7936, 256], P(None, 'ctx', 'tp'), may hold values from -4 to 4
- cache_lens: int32 [16], replicated, may hold values from 1 to 496, 3968 in all
- segment_ids: int32 [256], replicated, may hold values from 0 to 15, never falling along the last dimension, each value on 1 to 32 neighbouring positions
Outputs:
- attn_out: bfloat16 [256, 2048], P(('ctx', 'tp'))
- attn_lse: float32 [256, 16], P('ctx', 'tp')
Inputs may be any that keep to these rules, and one draw needn't show every extreme that they name: The filled slots of shard c are its first cache_lens[c] slots; the lengths sum to 3968 and some shard is full. `segment_ids`: never falls along the turn; a segment holds at most 32 tokens, and some segment exactly 32.
All inputs are finite; a program needn't handle non-finite values.
Results may differ from a plain program's by a relative error of at most 0.0015.
Values may be sent and summed in bfloat16 or wider, within the bound.
A program may use at most 64 MiB of HBM per device.

v0:
```python
import jax
import jax.numpy as jnp
from jax import lax
from jax.sharding import PartitionSpec as P


def shard_partial(queries, query_seg, keys_all, values_all, filled, key_seg, head_dim):
    rows = queries.shape[0]
    heads = queries.shape[1] // head_dim
    total = keys_all.shape[0]
    cache_count = total - key_seg.shape[0]
    flat = queries.reshape(rows * heads, head_dim)
    scores = lax.dot_general(
        flat, keys_all, (((1,), (1,)), ((), ())), preferred_element_type=jnp.float32
    ) * head_dim ** (-0.5)
    scores = scores.reshape(rows, heads, total)
    slot_rank = jnp.where(jnp.arange(cache_count) < filled, -1, 2**30).astype(jnp.int32)
    key_rank = jnp.concatenate([slot_rank, key_seg])
    visible = key_rank[None, None, :] <= query_seg[:, None, None]
    masked = jnp.where(visible, scores, -jnp.inf)
    peak = jnp.max(masked, axis=2)
    expo = jnp.exp(masked - peak[:, :, None])
    denom = jnp.sum(expo, axis=2)
    weights = expo.astype(jnp.bfloat16).reshape(rows * heads, total)
    mixed = jnp.dot(weights, values_all, preferred_element_type=jnp.float32)
    mixed = mixed.reshape(rows, heads, head_dim) / denom[:, :, None]
    return (mixed.reshape(rows, heads * head_dim), peak + jnp.log(denom))


def shards(q_new, kv_new, kv_cache, cache_lens, segment_ids):
    head_dim = kv_cache.shape[2]
    block = kv_new.shape[1]
    here = lax.axis_index("ctx")
    count = lax.axis_size("ctx")
    queries = lax.all_to_all(q_new, "tp", split_axis=1, concat_axis=0, tiled=True)
    heads = queries.shape[1] // head_dim
    keys_all = jnp.concatenate([kv_cache[0], kv_new[0]])
    values_all = jnp.concatenate([kv_cache[1], kv_new[1]])
    filled = cache_lens[here]
    key_seg = lax.dynamic_slice_in_dim(segment_ids, here * block, block, 0)
    total_rows = block * count
    init = (
        jnp.zeros((total_rows, heads * head_dim), jnp.float32),
        jnp.zeros((total_rows, heads), jnp.float32),
    )
    piece = lax.all_gather(queries, "ctx", axis=0, tiled=True)
    rows = piece.shape[0]
    width = 64

    def one_block(index, inner):
        outs, lses = inner
        offset = index * width
        part = lax.dynamic_slice_in_dim(piece, index * width, width, 0)
        part_seg = lax.dynamic_slice_in_dim(segment_ids, offset, width, 0)
        mixed, lse = shard_partial(part, part_seg, keys_all, values_all, filled, key_seg, head_dim)
        outs = lax.dynamic_update_slice_in_dim(outs, mixed, offset, 0)
        lses = lax.dynamic_update_slice_in_dim(lses, lse, offset, 0)
        return (outs, lses)

    partial_out, partial_lse = lax.fori_loop(0, rows // width, one_block, init)
    got_out, got_lse = (
        lax.all_to_all(
            partial_out.reshape(count, block, heads * head_dim),
            "ctx",
            split_axis=0,
            concat_axis=0,
            tiled=True,
        ),
        lax.all_to_all(
            partial_lse.reshape(count, block, heads), "ctx", split_axis=0, concat_axis=0, tiled=True
        ),
    )
    peak = jnp.max(got_lse, axis=0)
    scale = jnp.exp(got_lse - peak[None])
    denom = jnp.sum(scale, axis=0)
    numer = jnp.sum(got_out.reshape(count, block, heads, head_dim) * scale[:, :, :, None], axis=0)
    final = (numer / denom[:, :, None]).reshape(block, heads * head_dim)
    lse_out = peak + jnp.log(denom)
    attn_out = lax.all_to_all(
        final.astype(jnp.bfloat16), "tp", split_axis=0, concat_axis=1, tiled=True
    )
    return (attn_out, lse_out)


def solution(mesh):
    return jax.shard_map(
        shards,
        mesh=mesh,
        in_specs=(P(("ctx", "tp"), None), P(None, "ctx", "tp"), P(None, "ctx", "tp"), P(), P()),
        out_specs=(P(("ctx", "tp"), None), P("ctx", "tp")),
        check_vma=False,
    )
```

profile of v0, /device:TPU:0, one launch (start us, length us, event | category | flops | bytes accessed | tf_op | source)
XLA Modules:
  0.0 90.2 jit_solution(1802685320008893950)
XLA Ops:
  0.6 4.2 %all-to-all-start = ((bf16[8,2,1024]{2,0,1:T(8,128)(2,1)}), bf16[8,2,1024]{2,0,1:T(8,128)(2,1)S(1)}, u32[]{:S(2)}, u32[]{:S(2)}) async-start(bf16[8,2,1024]{2,0,1:T(8,128)(2,1)} %bitcast.58), calls=%async_computation | async-start | bytes 65536 | tf_op jit(solution)/shard_map/all_to_all | solution.py:35
  4.8 1.0 %slice_bitcast_fusion = (bf16[496,128]{1,0:T(8,128)(2,1)S(1)}, bf16[496,128]{1,0:T(8,128)(2,1)S(1)}) fusion(bf16[2,496,128]{2,1,0:T(8,128)(2,1)} %param.9), kind=kLoop, calls=%fused_computation.19 | loop fusion | bytes 507904 | tf_op jit(solution)/shard_map/squeeze | solution.py:38
  5.9 0.7 copy-done.1
  6.7 0.7 copy-done.2
  7.3 0.6 dynamic_slice.20
  7.9 0.9 all-to-all-done
  8.8 23.7 %all_gather.3 = bf16[256,1024]{1,0:T(8,128)(2,1)S(1)} all-gather(bf16[16,1024]{1,0:T(8,128)(2,1)S(1)} %bitcast.56), channel_id=1, replica_groups=mesh['ctx'=16,'tp'=2] {'ctx'}, dimensions={0}, use_global_device_ids=true | all-gather | bytes 557056 | tf_op jit(solution)/shard_map/all_gather | solution.py:46
  32.5 1.1 %broadcast_in_dim.61 = f32[256,1024]{1,0:T(8,128)} broadcast(f32[]{:T(128)} %constant.70.clone.1), dimensions={} | broadcast | bytes 1048580 | tf_op jit(solution)/shard_map/broadcast_in_dim | solution.py:43
  33.6 12.2 %while.15 = (s32[]{:T(128)}, f32[256,1024]{1,0:T(8,128)}, f32[256,8]{1,0:T(8,128)S(1)}, s32[]{:T(128)}, s32[16]{0:T(128)S(1)}, /*index=5*/s32[256]{0:T(256)S(1)}...) while((s32[]{:T(128)}, f32[256,1024]{1,0:T(8,128)}, ...), condition=%wide.region_3.4_spmd, body=%wide.region_0.3_spmd.sunk | while | flops 136152032 | bytes 5041023 | solution.py:60
  33.6 0.1 dynamic_slice.26
  33.7 0.6 fusion.24
  34.4 0.1 pad_add_fusion.2
  34.5 0.1 broadcast_compare_fusion.2
  34.6 0.4 fusion.25
  35.1 0.3 fusion.26
  35.4 0.1 div.49
  35.5 0.1 reduce_max.28
  35.6 0.4 convolution_divide_fusion.2
  35.9 0.7 bitcast_dynamic-update-slice_fusion.2
  36.8 0.6 fusion.24
  37.4 0.1 pad_add_fusion.2
  37.5 0.1 broadcast_compare_fusion.2
  37.7 0.4 fusion.25
  38.1 0.3 fusion.26
  38.4 0.1 div.49
  38.5 0.1 reduce_max.28
  38.6 0.4 convolution_divide_fusion.2
  39.0 0.8 bitcast_dynamic-update-slice_fusion.2
  39.8 0.6 fusion.24
  40.5 0.1 pad_add_fusion.2
  40.5 0.1 broadcast_compare_fusion.2
  40.7 0.4 fusion.25
  41.1 0.3 fusion.26
  41.5 0.1 div.49
  41.5 0.1 reduce_max.28
  41.7 0.4 convolution_divide_fusion.2
  42.0 0.8 bitcast_dynamic-update-slice_fusion.2
  42.9 0.6 fusion.24
  43.5 0.1 pad_add_fusion.2
  43.6 0.1 broadcast_compare_fusion.2
  43.8 0.4 fusion.25
  44.2 0.3 fusion.26
  44.5 0.1 div.49
  44.6 0.1 reduce_max.28
  44.7 0.4 convolution_divide_fusion.2
  45.1 0.8 bitcast_dynamic-update-slice_fusion.2
  45.8 0.1 copy.17
  45.9 0.1 reshape.108
  46.0 9.0 %all_to_all.45 = f32[16,1,128]{2,1,0:T(1,128)S(1)} all-to-all(f32[16,1,128]{2,1,0:T(1,128)S(1)} %reshape.108), channel_id=1, replica_groups=mesh['ctx'=16,'tp'=2] {'ctx'}, dimensions={0} | all-to-all | bytes 16384 | tf_op jit(solution)/shard_map/all_to_all | solution.py:69
  55.0 3.7 %all-to-all-start.1 = ((f32[16,16,1024]{2,1,0:T(8,128)}), f32[16,16,1024]{2,1,0:T(8,128)S(1)}, u32[]{:S(2)}, u32[]{:S(2)}) async-start(f32[16,16,1024]{2,1,0:T(8,128)} %bitcast.11), calls=%async_computation.1 | async-start | bytes 2097152 | tf_op jit(solution)/shard_map/all_to_all | solution.py:62
  58.7 0.5 broadcast.61
  59.2 0.7 reduce.7
  59.9 0.1 reshape.109
  60.1 0.1 copy.20
  60.2 0.3 mul.30
  60.6 0.2 mul.31
  60.8 0.1 div.36
  60.9 20.7 %all-to-all-done.1 = f32[16,16,1024]{2,1,0:T(8,128)S(1)} async-done(((f32[16,16,1024]{2,1,0:T(8,128)}), f32[16,16,1024]{2,1,0:T(8,128)S(1)}, u32[]{:S(2)}, u32[]{:S(2)}) %all-to-all-start.1) | async-done | bytes 1048608 | tf_op jit(solution)/shard_map/all_to_all | solution.py:62
  81.6 0.2 multiply_reduce_fusion
  81.7 0.6 fusion.8
  82.4 3.3 %all-to-all-start.3 = ((bf16[2,8,1024]{2,1,0:T(8,128)(2,1)}), bf16[2,8,1024]{2,1,0:T(8,128)(2,1)S(1)}, u32[]{:S(2)}, u32[]{:S(2)}) async-start(bf16[2,8,1024]{2,1,0:T(8,128)(2,1)} %fusion.8), calls=%async_computation.3 | async-start | bytes 65536 | tf_op jit(solution)/shard_map/all_to_all | solution.py:79
  85.6 0.7 copy.22
  86.3 3.3 %all-to-all-done.3 = bf16[2,8,1024]{2,1,0:T(8,128)(2,1)S(1)} async-done(((bf16[2,8,1024]{2,1,0:T(8,128)(2,1)}), bf16[2,8,1024]{2,1,0:T(8,128)(2,1)S(1)}, u32[]{:S(2)}, u32[]{:S(2)}) %all-to-all-start.3) | async-done | bytes 32800 | tf_op jit(solution)/shard_map/all_to_all | solution.py:79
  89.6 0.6 copy.43
  (29 shorter events, 1.0 us)
Async XLA Ops:
  0.6 8.2 %all-to-all-start = ((bf16[8,2,1024]{2,0,1:T(8,128)(2,1)}), bf16[8,2,1024]{2,0,1:T(8,128)(2,1)S(1)}, u32[]{:S(2)}, u32[]{:S(2)}) async-start(bf16[8,2,1024]{2,0,1:T(8,128)(2,1)} %bitcast.58), calls=%async_computation | async-start | bytes 65536 | tf_op jit(solution)/shard_map/all_to_all | solution.py:35
  4.8 1.0 %copy-start = (bf16[2,16,128]{2,1,0:T(8,128)(2,1)S(1)}, bf16[2,16,128]{2,1,0:T(8,128)(2,1)}, u32[]{:S(2)}) copy-start(bf16[2,16,128]{2,1,0:T(8,128)(2,1)} %param.8) | copy-start | bytes 24580
  5.9 0.7 copy-start.1
  6.7 0.7 copy-start.2
  55.0 26.6 %all-to-all-start.1 = ((f32[16,16,1024]{2,1,0:T(8,128)}), f32[16,16,1024]{2,1,0:T(8,128)S(1)}, u32[]{:S(2)}, u32[]{:S(2)}) async-start(f32[16,16,1024]{2,1,0:T(8,128)} %bitcast.11), calls=%async_computation.1 | async-start | bytes 2097152 | tf_op jit(solution)/shard_map/all_to_all | solution.py:62
  82.4 7.2 %all-to-all-start.3 = ((bf16[2,8,1024]{2,1,0:T(8,128)(2,1)}), bf16[2,8,1024]{2,1,0:T(8,128)(2,1)S(1)}, u32[]{:S(2)}, u32[]{:S(2)}) async-start(bf16[2,8,1024]{2,1,0:T(8,128)(2,1)} %fusion.8), calls=%async_computation.3 | async-start | bytes 65536 | tf_op jit(solution)/shard_map/all_to_all | solution.py:79
where the time goes:
time: 91.7 us; the launch traced here: 90.2 us
  blocking collectives  32.7 us (36%)
  waiting for transfers between devices  24.9 us (27%)
  local copies, waits for them, and re-layouts  11.3 us (12%)
  starting transfers between devices  11.1 us (12%)
  other arithmetic  6.06 us (7%)
  matrix products  3.1 us (3%)
    all_gather x1, blocking collectives, shards(): piece = lax.all_gather(queries, 'ctx', axis=0, tiled=True)  23.7 us
    all_to_all x1, waiting for transfers between devices, shards(): lax.all_to_all(partial_out.reshape(count, block, heads * head_dim), 'ctx'...  20.7 us
    all_to_all x1, blocking collectives, shards(): lax.all_to_all(partial_lse.reshape(count, block, heads), 'ctx', split_axi...  8.98 us
    all_to_all x1, starting transfers between devices, shards(): lax.all_to_all(q_new, 'tp', split_axis=1, concat_axis=0, tiled=True)  4.22 us
    all_to_all x1, starting transfers between devices, shards(): lax.all_to_all(partial_out.reshape(count, block, heads * head_dim), 'ctx'...  3.65 us
    all_to_all x1, starting transfers between devices, shards(): lax.all_to_all(final.astype(jnp.bfloat16), 'tp', split_axis=0, concat_axi...  3.26 us
    all_to_all x1, waiting for transfers between devices, shards(): lax.all_to_all(final.astype(jnp.bfloat16), 'tp', split_axis=0, concat_axi...  3.25 us
    dynamic_update_slice x4, local copies, waits for them, and re-layouts, one_block(): outs = lax.dynamic_update_slice_in_dim(outs, mixed, offset, 0)  3.02 us
  transfers between devices with their start and end apart: 3, of which 3 were waited for; matrix products, arithmetic and copies ran while one was open for 5% of the time, Pallas kernels for 0%

commit v1 on v0

v1 whole, which is shorter than its diff:
```python
import functools
import math

import jax
import jax.numpy as jnp
from jax import lax
from jax.experimental import pallas as pl
from jax.experimental.pallas import tpu as pltpu
from jax.sharding import PartitionSpec as P

GANG = 4


def kernel(
    H, T, R, scale,
    q_ref, cache_ref, new_ref, lens_ref, end_ref,
    out_ref, lse_ref,
    qbuf, kv, osend, orecv, acc, run, wcol, lsebuf,
    q_send, q_recv, kv_send, kv_recv, own_sem, o_send, o_recv,
):
    c2 = scale * math.log2(math.e)
    ctx, me = lax.axis_index("ctx"), lax.axis_index("tp")
    hi, lo = ctx // GANG, lax.rem(ctx, GANG)
    base = hi * GANG
    b0, b1 = lax.rem(lo, 2), lo // 2
    flip = [b1 * 2 + b0, b1 * 2 + 1 - b0, (1 - b1) * 2 + b0, (1 - b1) * 2 + 1 - b0]
    slots, block = cache_ref.shape[1], new_ref.shape[1]
    keys = slots + block

    def dev(c, t):
        return {"ctx": c, "tp": t}

    def peer(j):
        return lax.rem(hi + j + H, H) * GANG + lo

    def tpeer(i):
        return lax.rem(me + i + T, T)

    barrier = pltpu.get_barrier_semaphore()
    count = 0
    for j in range(H):
        for i in range(T):
            if j or i:
                pl.semaphore_signal(barrier, inc=1, device_id=dev(peer(j), tpeer(i)))
                count += 1
    for r in (1, 2):
        pl.semaphore_signal(barrier, inc=1, device_id=dev(base + flip[r], me))
        count += 1
    own = [
        pltpu.make_async_copy(cache_ref, kv.at[0, :, 0:slots], own_sem.at[0]),
        pltpu.make_async_copy(new_ref, kv.at[0, :, slots:keys], own_sem.at[1]),
    ]
    for copy in own:
        copy.start()
    pl.semaphore_wait(barrier, count)

    def kv_copies(r):
        target = dev(base + flip[r], me)
        return [
            pltpu.make_async_remote_copy(
                cache_ref, kv.at[r, :, 0:slots], kv_send.at[r, 0], kv_recv.at[r, 0], device_id=target),
            pltpu.make_async_remote_copy(
                new_ref, kv.at[r, :, slots:keys], kv_send.at[r, 1], kv_recv.at[r, 1], device_id=target),
        ]

    def q_copy(j, i):
        g = tpeer(i)
        return pltpu.make_async_remote_copy(
            q_ref.at[g], qbuf.at[j, me], q_send.at[j, i], q_recv.at[j, i],
            device_id=dev(peer(-j), g))

    def q_arrival(j, i):
        return pltpu.make_async_remote_copy(
            q_ref.at[me], qbuf.at[j, tpeer(-i)], q_send.at[j, i], q_recv.at[j, i],
            device_id=dev(peer(j), tpeer(-i)))

    far, near = kv_copies(2), kv_copies(1)
    for j in range(H):
        for i in range(T):
            if j or i:
                q_copy(j, i).start()
    for copy in far + near:
        copy.start()
    qbuf[0, me] = q_ref[me]
    for j in range(H):
        for i in range(T):
            if j or i:
                q_arrival(j, i).wait_recv()
    for copy in own:
        copy.wait()

    relay = pltpu.make_async_remote_copy(
        kv.at[2], kv.at[3], kv_send.at[3, 0], kv_recv.at[3, 0], device_id=dev(base + flip[1], me))

    def o_copy(j, i):
        t = tpeer(i)
        return pltpu.make_async_remote_copy(
            osend.at[j, t], orecv.at[j, me], o_send.at[j, i], o_recv.at[j, i],
            device_id=dev(peer(j), t))

    def o_arrival(j, i):
        return pltpu.make_async_remote_copy(
            osend.at[j, me], orecv.at[j, tpeer(-i)], o_send.at[j, i], o_recv.at[j, i],
            device_id=dev(peer(-j), tpeer(-i)))

    B = T * R
    group = 2 if H % 2 == 0 else 1
    width = group * B
    for r in range(GANG):
        if r == 1:
            for copy in near:
                copy.wait_recv()
        if r == 2:
            for copy in far:
                copy.wait_recv()
            relay.start()
        if r == 3:
            relay.wait_recv()
        shard = base + flip[r]
        filled = lens_ref[shard]
        for u in range(H // group):
            queries = qbuf[u * group:(u + 1) * group].reshape(width, q_ref.shape[2])
            ends = jnp.concatenate(
                [end_ref[pl.ds(peer(u * group + k), 1), :] for k in range(group)], axis=1)
            scores = lax.dot_general(
                kv[r, 0], queries, (((1,), (1,)), ((), ())), preferred_element_type=jnp.float32)
            old = scores[0:slots]
            spot = lax.broadcasted_iota(jnp.int32, old.shape, 0)
            old = jnp.where(spot < filled, old, -jnp.inf)
            fresh = scores[slots:keys]
            place = lax.broadcasted_iota(jnp.int32, fresh.shape, 0) + shard * block
            fresh = jnp.where(place < ends, fresh, -jnp.inf)
            masked = jnp.concatenate([old, fresh], axis=0)
            peak = jnp.max(masked, axis=0, keepdims=True)
            expo = jnp.exp2((masked - peak) * c2)
            total = jnp.sum(expo, axis=0, keepdims=True)
            mixed = lax.dot_general(
                kv[r, 1], expo.astype(jnp.bfloat16), (((0,), (0,)), ((), ())),
                preferred_element_type=jnp.float32)
            if r == 0:
                top, denom, numer = peak, total, mixed
            else:
                before = run[u, 0:1]
                top = jnp.maximum(before, peak)
                keep, add = jnp.exp2((before - top) * c2), jnp.exp2((peak - top) * c2)
                denom = run[u, 1:2] * keep + total * add
                numer = acc[u] * keep + mixed * add
            if r < GANG - 1:
                run[u, 0:1], run[u, 1:2] = top, denom
                acc[u] = numer
            else:
                rows = numer.T.reshape(group, T, R, q_ref.shape[2])
                for k in range(group):
                    j = u * group + k
                    osend[j, :, 0:R] = rows[k]
                    tops = jnp.broadcast_to(top[:, k * B:(k + 1) * B], (4, B))
                    denoms = jnp.broadcast_to(denom[:, k * B:(k + 1) * B], (4, B))
                    tail = jnp.concatenate([tops, denoms], axis=0)
                    for t in range(T):
                        osend[j, t, R:R + 8] = tail
                    for i in range(T):
                        if j or i:
                            o_copy(j, i).start()
    orecv[0, me] = osend[0, me]
    for j in range(H):
        for i in range(T):
            if j or i:
                o_arrival(j, i).wait_recv()
    for g in range(T):
        tops = [orecv[j, g, R:R + 1] for j in range(H)]
        top = functools.reduce(jnp.maximum, tops)
        ws = [jnp.exp2((x - top) * c2) for x in tops]
        total = sum(w * orecv[j, g, R + 4:R + 5] for j, w in enumerate(ws))
        lsebuf[g] = jnp.broadcast_to(top * scale + jnp.log(total), (8, B))
        inverse = 1.0 / total
        ws = [w * inverse for w in ws]
        ws += [jnp.zeros_like(top)] * (-H % 8)
        wcol[...] = jnp.concatenate(ws, axis=0).T
        cols = wcol[pl.ds(me * R, R), :]
        final = sum(cols[:, j:j + 1] * orecv[j, g, 0:R] for j in range(H))
        out_ref[g] = final.astype(out_ref.dtype)
    lse_ref[...] = lsebuf[me]
    for j in range(H):
        for i in range(T):
            if j or i:
                q_copy(j, i).wait_send()
                o_copy(j, i).wait_send()
    for copy in far + near + [relay]:
        copy.wait_send()


def shards(q_new, kv_new, kv_cache, cache_lens, segment_ids):
    hd = kv_cache.shape[2]
    block, slots = kv_new.shape[1], kv_cache.shape[1]
    tokens = q_new.shape[0]
    n, T = lax.axis_size("ctx"), lax.axis_size("tp")
    H = n // GANG
    heads = q_new.shape[1] // (hd * T)
    R = tokens * heads
    B = T * R
    hpad = H + (-H % 8)
    q = q_new.reshape(tokens, T, heads, hd).transpose(1, 0, 2, 3).reshape(T, R, hd)
    ends = jnp.sum((segment_ids[None, :] <= segment_ids[:, None]).astype(jnp.int32), axis=1)
    ends = jnp.repeat(ends, heads).reshape(n, B)
    vmem = pl.BlockSpec(memory_space=pltpu.VMEM)
    hbm = pl.BlockSpec(memory_space=pl.ANY)
    dma = pltpu.SemaphoreType.DMA
    out, lse = pl.pallas_call(
        functools.partial(kernel, H, T, R, hd ** -0.5),
        out_shape=(
            jax.ShapeDtypeStruct((T, R, hd), jnp.bfloat16),
            jax.ShapeDtypeStruct((8, B), jnp.float32),
        ),
        in_specs=[vmem, hbm, hbm, pl.BlockSpec(memory_space=pltpu.SMEM), vmem],
        out_specs=(vmem, vmem),
        scratch_shapes=[
            pltpu.VMEM((H, T, R, hd), jnp.bfloat16),
            pltpu.VMEM((GANG, 2, slots + block, hd), jnp.bfloat16),
            pltpu.VMEM((H, T, R + 8, hd), jnp.float32),
            pltpu.VMEM((H, T, R + 8, hd), jnp.float32),
            pltpu.VMEM((H // 2 if H % 2 == 0 else H, hd, 2 * B if H % 2 == 0 else B), jnp.float32),
            pltpu.VMEM((H // 2 if H % 2 == 0 else H, 8, 2 * B if H % 2 == 0 else B), jnp.float32),
            pltpu.VMEM((B, hpad), jnp.float32),
            pltpu.VMEM((T, 8, B), jnp.float32),
            dma((H, T)), dma((H, T)), dma((GANG, 2)), dma((GANG, 2)), dma((2,)), dma((H, T)), dma((H, T)),
        ],
        compiler_params=pltpu.CompilerParams(
            collective_id=0, has_side_effects=True, vmem_limit_bytes=48 * 2 ** 20),
    )(q, kv_cache, kv_new, cache_lens, ends)
    attn = out.reshape(T, tokens, heads, hd).transpose(1, 0, 2, 3).reshape(tokens, T * heads * hd)
    return attn, lse[0].reshape(block, heads)


def solution(mesh):
    return jax.shard_map(
        shards,
        mesh=mesh,
        in_specs=(P(("ctx", "tp"), None), P(None, "ctx", "tp"), P(None, "ctx", "tp"), P(), P()),
        out_specs=(P(("ctx", "tp"), None), P("ctx", "tp")),
        check_vma=False,
    )
```

time: 91.7 us -> 29.5 us (0.32); the launches traced: 90.2 us -> 29.3 us
  blocking collectives: 32.7 us -> 0 us
  waiting for transfers between devices: 24.9 us -> 0 us
  Pallas kernels: 0 us -> 23.7 us
  starting transfers between devices: 11.1 us -> 0 us
  local copies, waits for them, and re-layouts: 11.3 us -> 3.95 us
  other arithmetic: 6.06 us -> 0.93 us
  matrix products: 3.1 us -> 0 us
    all_to_all x3 -> x0, waiting for transfers between devices: 24.9 us -> none  [the longest x1 20.7 us: shards(): lax.all_to_all(partial_out.reshape(count, block, heads * head_dim), 'ctx'...]
    pallas_call x0 -> x1, Pallas kernels: none -> 23.7 us  [shards(): pl.pallas_call(functools.partial(kernel, H, T, R, hd ** (-0.5)), out_shap...]
    all_gather x1 -> x0, blocking collectives: 23.7 us -> none  [shards(): piece = lax.all_gather(queries, 'ctx', axis=0, tiled=True)]
    all_to_all x3 -> x0, starting transfers between devices: 11.1 us -> none  [the longest x1 4.22 us: shards(): lax.all_to_all(q_new, 'tp', split_axis=1, concat_axis=0, tiled=True)]
    all_to_all x1 -> x0, blocking collectives: 8.98 us -> none  [shards(): lax.all_to_all(partial_lse.reshape(count, block, heads), 'ctx', split_axi...]
    dot_general x8 -> x0, matrix products: 3.1 us -> none  [the longest x4 1.66 us: shard_partial(): lax.dot_general(flat, keys_all, (((1,), (1,)), ((), ())), preferred_eleme...]
    dynamic_update_slice x4 -> x0, local copies, waits for them, and re-layouts: 3.02 us -> none  [one_block(): outs = lax.dynamic_update_slice_in_dim(outs, mixed, offset, 0)]
    select_n x4 -> x0, other arithmetic: 2.59 us -> none  [shard_partial(): jnp.where(jnp.arange(cache_count) < filled, -1, 2 ** 30).astype(jnp.int32)]
  transfers between devices with their start and end apart: 3 -> 0, of which waited for: 3 -> 0; matrix products, arithmetic and copies ran while one was open for 5% -> 0% of each run, Pallas kernels for 0% -> 0%
where the time goes in v1:
time: 29.5 us; the launch traced here: 29.3 us
  Pallas kernels  23.7 us (80%)
  local copies, waits for them, and re-layouts  3.95 us (13%)
  other arithmetic  0.93 us (3%)
  between operations  0.66 us (2%)
    pallas_call x1, Pallas kernels, shards(): pl.pallas_call(functools.partial(kernel, H, T, R, hd ** (-0.5)), out_shap...  23.7 us
    unnamed x9, local copies, waits for them, and re-layouts  3.02 us
    reduce_sum x1, other arithmetic, shards(): jnp.sum((segment_ids[None, :] <= segment_ids[:, None]).astype(jnp.int32),...  0.93 us
    transpose x1, local copies, waits for them, and re-layouts, shards(): out.reshape(T, tokens, heads, hd).transpose(1, 0, 2, 3)  0.62 us

profile of v1, /device:TPU:0, one launch (start us, length us, event | category | flops | bytes accessed | tf_op | source)
XLA Modules:
  0.0 29.3 jit_solution(490318620882777520)
XLA Ops:
  0.6 0.9 %convert_reduce_fusion = s32[256]{0:T(256)S(1)} fusion(s32[256]{0:T(256)} %param.9), kind=kLoop, calls=%fused_computation | loop fusion | flops 196352 | bytes 2048 | tf_op jit(solution)/shard_map/reduce_sum | solution.py:203
  1.6 0.1 broadcast_in_dim.9
  1.6 0.1 copy.20
  1.7 0.0 copy-start.3
  1.7 0.1 copy.21.end_ref
  1.8 0.7 %copy-done.3 = bf16[8,2048]{1,0:T(8,128)(2,1)S(1)} copy-done((bf16[8,2048]{1,0:T(8,128)(2,1)S(1)}, bf16[8,2048]{1,0:T(8,128)(2,1)}, u32[]{:S(2)}) %copy-start.3) | copy-done | bytes 32792
  2.5 0.0 copy-start.1
  2.5 0.0 copy-start.2
  2.5 0.7 %copy-done.1 = bf16[2,16,128]{2,1,0:T(8,128)(2,1)S(1)} copy-done((bf16[2,16,128]{2,1,0:T(8,128)(2,1)S(1)}, bf16[2,16,128]{2,1,0:T(8,128)(2,1)}, u32[]{:S(2)}) %copy-start.1) | copy-done | bytes 8216
  3.2 0.0 copy-done.2
  3.2 0.0 copy-start
  3.2 0.9 %copy-done = bf16[2,496,128]{2,1,0:T(8,128)(2,1)S(1)} copy-done((bf16[2,496,128]{2,1,0:T(8,128)(2,1)S(1)}, bf16[2,496,128]{2,1,0:T(8,128)(2,1)}, u32[]{:S(2)}) %copy-start) | copy-done | bytes 253976
  4.1 23.7 %shard_map.68 = (bf16[2,64,128]{2,1,0:T(8,128)(2,1)S(1)}, f32[8,128]{1,0:T(8,128)S(1)}) custom-call(bf16[2,64,128]{2,1,0:T(8,128)(2,1)S(1)} %bitcast.12, bf16[2,496,128]{2,1,0:T(8,128)(2,1)S(1)} %copy-done, bf16[2,16,128]{2,1,0:T(8,128)(2,1)S(1)} %copy-done.1, s32[16]{0:T(128)S(1)} %copy-done.2, s32[16,128]{1,0:T(8,128)S(1)} %copy.21.end_ref), custom_call_target="tpu_custom_call" | custom-call | tf_op jit(solution)/shard_map/pallas_call | solution.py:208
  27.9 0.6 %copy.22 = bf16[8,2,8,128]{3,0,2,1:T(8,128)(2,1)} copy(bf16[8,2,8,128]{3,2,0,1:T(8,128)(2,1)S(1)} %bitcast.13) | data formatting | bytes 65536 | tf_op jit(solution)/shard_map/transpose | solution.py:230
  28.5 0.1 reshape_squeeze.3
  28.6 0.7 %copy.23 = f32[16,8]{0,1:T(8,128)} copy(f32[16,8]{1,0:T(8,128)S(1)} %reshape_squeeze.3) | data formatting | bytes 1024
  (3 shorter events, 0.0 us)
Async XLA Ops:
  1.7 0.8 %copy-start.3 = (bf16[8,2048]{1,0:T(8,128)(2,1)S(1)}, bf16[8,2048]{1,0:T(8,128)(2,1)}, u32[]{:S(2)}) copy-start(bf16[8,2048]{1,0:T(8,128)(2,1)} %param.5) | copy-start | bytes 98308
  2.5 0.7 %copy-start.1 = (bf16[2,16,128]{2,1,0:T(8,128)(2,1)S(1)}, bf16[2,16,128]{2,1,0:T(8,128)(2,1)}, u32[]{:S(2)}) copy-start(bf16[2,16,128]{2,1,0:T(8,128)(2,1)} %new_ref.1) | copy-start | bytes 24580
  2.5 0.7 %copy-start.2 = (s32[16]{0:T(128)S(1)}, s32[16]{0:T(128)}, u32[]{:S(2)}) copy-start(s32[16]{0:T(128)} %lens_ref.1) | copy-start | bytes 196
  3.2 0.9 %copy-start = (bf16[2,496,128]{2,1,0:T(8,128)(2,1)S(1)}, bf16[2,496,128]{2,1,0:T(8,128)(2,1)}, u32[]{:S(2)}) copy-start(bf16[2,496,128]{2,1,0:T(8,128)(2,1)} %cache_ref.1) | copy-start | bytes 761860

commit v2 on v1

v2 whole, which is shorter than its diff:
```python
import functools
import math

import jax
import jax.numpy as jnp
from jax import lax
from jax.experimental import pallas as pl
from jax.experimental.pallas import tpu as pltpu
from jax.sharding import PartitionSpec as P

TINY, STEPS = 1e-30, 32767.0
GANG = 4


def kernel(
    H, T, R, scale,
    q_hbm, cache_ref, new_ref, lens_hbm, seg_hbm,
    out_ref, lse_ref,
    qraw, q_ref, lens_ref, segrow, segcol, qseg,
    qbuf, kv, osend, orecv, ssend, srecv, acc, run, wcol, lsebuf,
    q_send, q_recv, kv_send, kv_recv, own_sem, o_send, o_recv, s_send, s_recv,
):
    c2 = scale * math.log2(math.e)
    ctx, me = lax.axis_index("ctx"), lax.axis_index("tp")
    hi, lo = ctx // GANG, lax.rem(ctx, GANG)
    base = hi * GANG
    b0, b1 = lax.rem(lo, 2), lo // 2
    flip = [b1 * 2 + b0, b1 * 2 + 1 - b0, (1 - b1) * 2 + b0, (1 - b1) * 2 + 1 - b0]
    slots, block = cache_ref.shape[1], new_ref.shape[1]
    keys = slots + block
    tokens, hd = qraw.shape[0], cache_ref.shape[2]
    heads, B = R // tokens, T * R

    def dev(c, t):
        return {"ctx": c, "tp": t}

    def peer(j):
        return lax.rem(hi + j + H, H) * GANG + lo

    def tpeer(i):
        return lax.rem(me + i + T, T)

    barrier = pltpu.get_barrier_semaphore()
    count = 0
    for j in range(H):
        for i in range(T):
            if j or i:
                pl.semaphore_signal(barrier, inc=1, device_id=dev(peer(j), tpeer(i)))
                count += 1
    for r in (1, 2):
        pl.semaphore_signal(barrier, inc=1, device_id=dev(base + flip[r], me))
        count += 1
    local = [
        pltpu.make_async_copy(q_hbm, qraw, own_sem.at[0]),
        pltpu.make_async_copy(seg_hbm, segrow, own_sem.at[1]),
        pltpu.make_async_copy(lens_hbm, lens_ref, own_sem.at[2]),
        pltpu.make_async_copy(new_ref, kv.at[0, :, slots:keys], own_sem.at[3]),
        pltpu.make_async_copy(cache_ref, kv.at[0, :, 0:slots], own_sem.at[4]),
    ]
    for copy in local:
        copy.start()
    local[0].wait()
    for g in range(T):
        first = g * heads * hd
        wide = qraw[:, first:first + heads * hd].astype(jnp.float32)
        q_ref[g] = jnp.concatenate(
            [wide[:, h * hd:(h + 1) * hd] for h in range(heads)], axis=0).astype(jnp.bfloat16)
    local[1].wait()
    total_new = segrow.shape[1]
    segcol[...] = jnp.broadcast_to(segrow[...].astype(jnp.float32), (8, total_new)).T
    lane = lax.broadcasted_iota(jnp.int32, (1, B), 1)
    inside = lax.div(lane, jnp.int32(R)) * tokens + lax.rem(lane, jnp.int32(tokens))
    token = lax.broadcasted_iota(jnp.int32, (total_new, B), 0)
    for j in range(H):
        here = token == inside + peer(j) * block
        qseg[j:j + 1] = jnp.sum(jnp.where(here, segcol[:, 0:1], 0.0), axis=0, keepdims=True)
    for copy in local[2:]:
        copy.wait()
    pl.semaphore_wait(barrier, count)

    def q_copy(j, i):
        g = tpeer(i)
        return pltpu.make_async_remote_copy(
            q_ref.at[g], qbuf.at[j, me], q_send.at[j, i], q_recv.at[j, i],
            device_id=dev(peer(-j), g))

    def q_arrival(j, i):
        return pltpu.make_async_remote_copy(
            q_ref.at[me], qbuf.at[j, tpeer(-i)], q_send.at[j, i], q_recv.at[j, i],
            device_id=dev(peer(j), tpeer(-i)))

    def kv_copy(source, slot, part, hop):
        return pltpu.make_async_remote_copy(
            kv.at[source, part], kv.at[slot, part], kv_send.at[slot, part], kv_recv.at[slot, part],
            device_id=dev(base + flip[hop], me))

    far = [kv_copy(0, 2, part, 2) for part in range(2)]
    near = [kv_copy(0, 1, part, 1) for part in range(2)]
    relay = [kv_copy(2, 3, part, 1) for part in range(2)]
    for j in range(H):
        for i in range(T):
            if j or i:
                q_copy(j, i).start()
    for copy in far + near:
        copy.start()
    qbuf[0, me] = q_ref[me]
    for j in range(H):
        for i in range(T):
            if j or i:
                q_arrival(j, i).wait_recv()

    def o_copy(j, i):
        t = tpeer(i)
        return pltpu.make_async_remote_copy(
            osend.at[j, t], orecv.at[j, me], o_send.at[j, i], o_recv.at[j, i],
            device_id=dev(peer(j), t))

    def o_arrival(j, i):
        return pltpu.make_async_remote_copy(
            osend.at[j, me], orecv.at[j, tpeer(-i)], o_send.at[j, i], o_recv.at[j, i],
            device_id=dev(peer(-j), tpeer(-i)))

    def s_copy(j, i):
        return pltpu.make_async_remote_copy(
            ssend.at[j], srecv.at[j, me], s_send.at[j, i], s_recv.at[j, i],
            device_id=dev(peer(j), tpeer(i)))

    def s_arrival(j, i):
        return pltpu.make_async_remote_copy(
            ssend.at[j], srecv.at[j, tpeer(-i)], s_send.at[j, i], s_recv.at[j, i],
            device_id=dev(peer(-j), tpeer(-i)))

    group = 2 if H % 2 == 0 else 1
    width = group * B
    for r in range(GANG):
        if r == 1:
            for copy in near:
                copy.wait_recv()
        if r == 2:
            for copy, onward in zip(far, relay):
                copy.wait_recv()
                onward.start()
        if r == 3:
            for copy in relay:
                copy.wait_recv()
        shard = base + flip[r]
        filled = lens_ref[shard]
        for u in range(H // group):
            queries = qbuf[u * group:(u + 1) * group].reshape(width, q_ref.shape[2])
            asks = jnp.concatenate(
                [qseg[u * group + k:u * group + k + 1] for k in range(group)], axis=1)
            scores = lax.dot_general(
                kv[r, 0], queries, (((1,), (1,)), ((), ())), preferred_element_type=jnp.float32)
            old = scores[0:slots]
            spot = lax.broadcasted_iota(jnp.int32, old.shape, 0)
            old = jnp.where(spot < filled, old, -jnp.inf)
            fresh = scores[slots:keys]
            theirs = segcol[pl.ds(pl.multiple_of(shard * block, block), block), 0:1]
            fresh = jnp.where(theirs <= asks, fresh, -jnp.inf)
            masked = jnp.concatenate([old, fresh], axis=0)
            peak = jnp.max(masked, axis=0, keepdims=True)
            expo = jnp.exp2((masked - peak) * c2)
            total = jnp.sum(expo, axis=0, keepdims=True)
            mixed = lax.dot_general(
                kv[r, 1], expo.astype(jnp.bfloat16), (((0,), (0,)), ((), ())),
                preferred_element_type=jnp.float32)
            if r == 0:
                top, denom, numer = peak, total, mixed
            else:
                before = run[u, 0:1]
                top = jnp.maximum(before, peak)
                keep, add = jnp.exp2((before - top) * c2), jnp.exp2((peak - top) * c2)
                denom = run[u, 1:2] * keep + total * add
                numer = acc[u] * keep + mixed * add
            if r < GANG - 1:
                run[u, 0:1], run[u, 1:2] = top, denom
                acc[u] = numer
            else:
                most = jnp.maximum(jnp.max(jnp.abs(numer), axis=0, keepdims=True), TINY)
                level = jnp.round(numer * (STEPS / most))
                rows = level.T.astype(jnp.int32).astype(jnp.int16).reshape(group, T, R, hd)
                for k in range(group):
                    j = u * group + k
                    osend[j] = rows[k]
                    stats = [x[:, k * B:(k + 1) * B] for x in (top, denom, most)]
                    ssend[j] = jnp.concatenate(stats + stats[:1] * 5, axis=0)
                    for i in range(T):
                        if j or i:
                            s_copy(j, i).start()
                            o_copy(j, i).start()
    orecv[0, me] = osend[0, me]
    srecv[0, me] = ssend[0]
    for j in range(H):
        for i in range(T):
            if j or i:
                s_arrival(j, i).wait_recv()
                o_arrival(j, i).wait_recv()
    for g in range(T):
        tops = [srecv[j, g, 0:1] for j in range(H)]
        top = functools.reduce(jnp.maximum, tops)
        ws = [jnp.exp2((x - top) * c2) for x in tops]
        total = sum(w * srecv[j, g, 1:2] for j, w in enumerate(ws))
        lsebuf[g] = jnp.broadcast_to(top * scale + jnp.log(total), (8, B))
        inverse = 1.0 / (total * STEPS)
        ws = [w * srecv[j, g, 2:3] * inverse for j, w in enumerate(ws)]
        ws += [jnp.zeros_like(top)] * (-H % 8)
        wcol[...] = jnp.concatenate(ws, axis=0).T
        cols = wcol[pl.ds(me * R, R), :]
        final = sum(
            cols[:, j:j + 1] * orecv[j, g].astype(jnp.int32).astype(jnp.float32) for j in range(H))
        first = g * heads * hd
        out_ref[:, first:first + heads * hd] = jnp.concatenate(
            [final[h * tokens:(h + 1) * tokens] for h in range(heads)], axis=1).astype(out_ref.dtype)
    lse_ref[...] = lsebuf[me]
    for j in range(H):
        for i in range(T):
            if j or i:
                q_copy(j, i).wait_send()
                s_copy(j, i).wait_send()
                o_copy(j, i).wait_send()
    for copy in far + near + relay:
        copy.wait_send()


def shards(q_new, kv_new, kv_cache, cache_lens, segment_ids):
    hd = kv_cache.shape[2]
    block, slots = kv_new.shape[1], kv_cache.shape[1]
    tokens = q_new.shape[0]
    n, T = lax.axis_size("ctx"), lax.axis_size("tp")
    H = n // GANG
    heads = q_new.shape[1] // (hd * T)
    R = tokens * heads
    B = T * R
    hpad = H + (-H % 8)
    vmem = pl.BlockSpec(memory_space=pltpu.VMEM)
    hbm = pl.BlockSpec(memory_space=pltpu.HBM)
    group = 2 if H % 2 == 0 else 1
    new = segment_ids.shape[0]
    dma = pltpu.SemaphoreType.DMA
    out, lse = pl.pallas_call(
        functools.partial(kernel, H, T, R, hd ** -0.5),
        out_shape=(
            jax.ShapeDtypeStruct(q_new.shape, jnp.bfloat16),
            jax.ShapeDtypeStruct((8, B), jnp.float32),
        ),
        in_specs=[hbm] * 5,
        out_specs=(vmem, vmem),
        scratch_shapes=[
            pltpu.VMEM(q_new.shape, jnp.bfloat16),
            pltpu.VMEM((T, R, hd), jnp.bfloat16),
            pltpu.SMEM(cache_lens.shape, jnp.int32),
            pltpu.VMEM((1, new), jnp.int32),
            pltpu.VMEM((new, 8), jnp.float32),
            pltpu.VMEM((H, B), jnp.float32),
            pltpu.VMEM((H, T, R, hd), jnp.bfloat16),
            pltpu.VMEM((GANG, 2, slots + block, hd), jnp.bfloat16),
            pltpu.VMEM((H, T, R, hd), jnp.int16),
            pltpu.VMEM((H, T, R, hd), jnp.int16),
            pltpu.VMEM((H, 8, B), jnp.float32),
            pltpu.VMEM((H, T, 8, B), jnp.float32),
            pltpu.VMEM((H // group, hd, group * B), jnp.float32),
            pltpu.VMEM((H // group, 8, group * B), jnp.float32),
            pltpu.VMEM((B, hpad), jnp.float32),
            pltpu.VMEM((T, 8, B), jnp.float32),
            dma((H, T)), dma((H, T)), dma((GANG, 2)), dma((GANG, 2)), dma((5,)), dma((H, T)), dma((H, T)), dma((H, T)), dma((H, T)),
        ],
        compiler_params=pltpu.CompilerParams(
            collective_id=0, has_side_effects=True, vmem_limit_bytes=48 * 2 ** 20),
    )(q_new, kv_cache, kv_new, cache_lens, segment_ids.reshape(1, new))
    lse = lse[0].reshape(T, heads, tokens).transpose(0, 2, 1).reshape(block, heads)
    return out, lse


def solution(mesh):
    return jax.shard_map(
        shards,
        mesh=mesh,
        in_specs=(P(("ctx", "tp"), None), P(None, "ctx", "tp"), P(None, "ctx", "tp"), P(), P()),
        out_specs=(P(("ctx", "tp"), None), P("ctx", "tp")),
        check_vma=False,
    )
```

time: 29.5 us -> 26.7 us (0.905)
  Pallas kernels: 23.7 us -> 21.3 us
  other arithmetic: 0.93 us -> 0 us
  local copies, waits for them, and re-layouts: 3.95 us -> 4.46 us
    pallas_call x1, Pallas kernels: 23.7 us -> 21.3 us  [shards(): pl.pallas_call(functools.partial(kernel, H, T, R, hd ** (-0.5)), out_shap...]
    reduce_sum x1 -> x0, other arithmetic: 0.93 us -> none  [shards(): jnp.sum((segment_ids[None, :] <= segment_ids[:, None]).astype(jnp.int32),...]
    reshape x1, local copies, waits for them, and re-layouts: 0.01 us -> 0.67 us  [shards(): lse[0].reshape(T, heads, tokens).transpose(0, 2, 1).reshape(block, heads)]
    unnamed x9 -> x11, local copies, waits for them, and re-layouts: 3.02 us -> 3.68 us
    transpose x1, local copies, waits for them, and re-layouts: 0.62 us -> 0.01 us  [shards(): lse[0].reshape(T, heads, tokens).transpose(0, 2, 1).reshape(block, heads)]
where the time goes in v2:
time: 26.7 us; the launch traced here: 26.4 us
  Pallas kernels  21.3 us (80%)
  local copies, waits for them, and re-layouts  4.46 us (17%)
  between operations  0.67 us (3%)
    pallas_call x1, Pallas kernels, shards(): pl.pallas_call(functools.partial(kernel, H, T, R, hd ** (-0.5)), out_shap...  21.3 us
    unnamed x11, local copies, waits for them, and re-layouts  3.68 us
    reshape x1, local copies, waits for them, and re-layouts, shards(): lse[0].reshape(T, heads, tokens).transpose(0, 2, 1).reshape(block, heads)  0.67 us

profile of v2, /device:TPU:0, one launch (start us, length us, event | category | flops | bytes accessed | tf_op | source)
XLA Modules:
  0.0 26.4 jit_solution(11540682128068205503)
XLA Ops:
  0.6 0.0 copy-start.3
  0.6 0.0 copy-start.4
  0.7 0.7 %copy-done.3 = s32[256]{0:T(256)S(1)} copy-done((s32[256]{0:T(256)S(1)}, s32[256]{0:T(256)}, u32[]{:S(2)}) %copy-start.3) | copy-done | bytes 1048
  1.3 0.0 copy-done.4
  1.3 0.0 copy-start
  1.3 0.9 %copy-done = bf16[2,496,128]{2,1,0:T(8,128)(2,1)S(1)} copy-done((bf16[2,496,128]{2,1,0:T(8,128)(2,1)S(1)}, bf16[2,496,128]{2,1,0:T(8,128)(2,1)}, u32[]{:S(2)}) %copy-start) | copy-done | bytes 253976
  2.3 0.0 copy-start.1
  2.3 0.8 %copy-done.1 = bf16[8,2048]{1,0:T(8,128)(2,1)S(1)} copy-done((bf16[8,2048]{1,0:T(8,128)(2,1)S(1)}, bf16[8,2048]{1,0:T(8,128)(2,1)}, u32[]{:S(2)}) %copy-start.1) | copy-done | bytes 32792
  3.0 0.0 copy-start.2
  3.0 0.7 %copy-done.2 = bf16[2,16,128]{2,1,0:T(8,128)(2,1)S(1)} copy-done((bf16[2,16,128]{2,1,0:T(8,128)(2,1)S(1)}, bf16[2,16,128]{2,1,0:T(8,128)(2,1)}, u32[]{:S(2)}) %copy-start.2) | copy-done | bytes 8216
  3.7 21.3 %shard_map.68 = (bf16[8,2048]{1,0:T(8,128)(2,1)S(1)}, f32[8,128]{1,0:T(8,128)S(1)}) custom-call(bf16[8,2048]{1,0:T(8,128)(2,1)S(1)} %copy-done.1, bf16[2,496,128]{2,1,0:T(8,128)(2,1)S(1)} %copy-done, bf16[2,16,128]{2,1,0:T(8,128)(2,1)S(1)} %copy-done.2, s32[16]{0:T(128)S(1)} %copy-done.4, s32[1,256]{1,0:T(1,128)S(1)} %bitcast.4), custom_call_target="tpu_custom_call" | custom-call | tf_op jit(solution)/shard_map/pallas_call | solution.py:240
  25.0 0.1 reshape_squeeze.3
  25.1 0.7 %reshape.11 = f32[16,8]{0,1:T(8,128)} reshape(f32[2,8,8]{1,0,2:T(2,128)S(1)} %copy.7) | data formatting | bytes 1024 | tf_op jit(solution)/shard_map/reshape | solution.py:270
  25.8 0.6 %copy.9 = bf16[8,2048]{1,0:T(8,128)(2,1)} copy(bf16[8,2048]{1,0:T(8,128)(2,1)S(1)} %get-tuple-element.8) | data formatting | bytes 65536
  (2 shorter events, 0.0 us)
Async XLA Ops:
  0.6 0.7 %copy-start.3 = (s32[256]{0:T(256)S(1)}, s32[256]{0:T(256)}, u32[]{:S(2)}) copy-start(s32[256]{0:T(256)} %param.9) | copy-start | bytes 3076
  0.6 0.7 %copy-start.4 = (s32[16]{0:T(128)S(1)}, s32[16]{0:T(128)}, u32[]{:S(2)}) copy-start(s32[16]{0:T(128)} %lens_hbm.1) | copy-start | bytes 196
  1.3 0.9 %copy-start = (bf16[2,496,128]{2,1,0:T(8,128)(2,1)S(1)}, bf16[2,496,128]{2,1,0:T(8,128)(2,1)}, u32[]{:S(2)}) copy-start(bf16[2,496,128]{2,1,0:T(8,128)(2,1)} %cache_ref.1) | copy-start | bytes 761860
  2.3 0.8 %copy-start.1 = (bf16[8,2048]{1,0:T(8,128)(2,1)S(1)}, bf16[8,2048]{1,0:T(8,128)(2,1)}, u32[]{:S(2)}) copy-start(bf16[8,2048]{1,0:T(8,128)(2,1)} %q_hbm.1) | copy-start | bytes 98308
  3.0 0.7 %copy-start.2 = (bf16[2,16,128]{2,1,0:T(8,128)(2,1)S(1)}, bf16[2,16,128]{2,1,0:T(8,128)(2,1)}, u32[]{:S(2)}) copy-start(bf16[2,16,128]{2,1,0:T(8,128)(2,1)} %new_ref.1) | copy-start | bytes 24580

commit v3 on v2

--- a/solution.py
+++ b/solution.py
@@ -132,62 +132,64 @@
 
     group = 2 if H % 2 == 0 else 1
     width = group * B
-    for r in range(GANG):
-        if r == 1:
-            for copy in near:
-                copy.wait_recv()
-        if r == 2:
-            for copy, onward in zip(far, relay):
-                copy.wait_recv()
-                onward.start()
-        if r == 3:
-            for copy in relay:
-                copy.wait_recv()
+    units = H // group
+    order = [(r, u) for r in (0, 1) for u in range(units)] + [(r, u) for u in range(units) for r in (2, 3)]
+    for r, u in order:
+        if u == 0:
+            if r == 1:
+                for copy in near:
+                    copy.wait_recv()
+            if r == 2:
+                for copy, onward in zip(far, relay):
+                    copy.wait_recv()
+                    onward.start()
+            if r == 3:
+                for copy in relay:
+                    copy.wait_recv()
         shard = base + flip[r]
         filled = lens_ref[shard]
-        for u in range(H // group):
-            queries = qbuf[u * group:(u + 1) * group].reshape(width, q_ref.shape[2])
-            asks = jnp.concatenate(
-                [qseg[u * group + k:u * group + k + 1] for k in range(group)], axis=1)
-            scores = lax.dot_general(
-                kv[r, 0], queries, (((1,), (1,)), ((), ())), preferred_element_type=jnp.float32)
-            old = scores[0:slots]
-            spot = lax.broadcasted_iota(jnp.int32, old.shape, 0)
-            old = jnp.where(spot < filled, old, -jnp.inf)
-            fresh = scores[slots:keys]
-            theirs = segcol[pl.ds(pl.multiple_of(shard * block, block), block), 0:1]
-            fresh = jnp.where(theirs <= asks, fresh, -jnp.inf)
-            masked = jnp.concatenate([old, fresh], axis=0)
-            peak = jnp.max(masked, axis=0, keepdims=True)
-            expo = jnp.exp2((masked - peak) * c2)
-            total = jnp.sum(expo, axis=0, keepdims=True)
-            mixed = lax.dot_general(
-                kv[r, 1], expo.astype(jnp.bfloat16), (((0,), (0,)), ((), ())),
-                preferred_element_type=jnp.float32)
-            if r == 0:
-                top, denom, numer = peak, total, mixed
-            else:
-                before = run[u, 0:1]
-                top = jnp.maximum(before, peak)
-                keep, add = jnp.exp2((before - top) * c2), jnp.exp2((peak - top) * c2)
-                denom = run[u, 1:2] * keep + total * add
-                numer = acc[u] * keep + mixed * add
-            if r < GANG - 1:
-                run[u, 0:1], run[u, 1:2] = top, denom
-                acc[u] = numer
-            else:
-                most = jnp.maximum(jnp.max(jnp.abs(numer), axis=0, keepdims=True), TINY)
-                level = jnp.round(numer * (STEPS / most))
-                rows = level.T.astype(jnp.int32).astype(jnp.int16).reshape(group, T, R, hd)
-                for k in range(group):
-                    j = u * group + k
-                    osend[j] = rows[k]
-                    stats = [x[:, k * B:(k + 1) * B] for x in (top, denom, most)]
-                    ssend[j] = jnp.concatenate(stats + stats[:1] * 5, axis=0)
-                    for i in range(T):
-                        if j or i:
-                            s_copy(j, i).start()
-                            o_copy(j, i).start()
+        queries = qbuf[u * group:(u + 1) * group].reshape(width, q_ref.shape[2])
+        asks = jnp.concatenate(
+            [qseg[u * group + k:u * group + k + 1] for k in range(group)], axis=1)
+        scores = lax.dot_general(
+            kv[r, 0], queries, (((1,), (1,)), ((), ())), preferred_element_type=jnp.float32)
+        old = scores[0:slots]
+        spot = lax.broadcasted_iota(jnp.int32, old.shape, 0)
+        old = jnp.where(spot < filled, old, -jnp.inf)
+        fresh = scores[slots:keys]
+        theirs = segcol[pl.ds(pl.multiple_of(shard * block, block), block), 0:1]
+        fresh = jnp.where(theirs <= asks, fresh, -jnp.inf)
+        masked = jnp.concatenate([old, fresh], axis=0)
+        peak = jnp.max(masked, axis=0, keepdims=True)
+        expo = jnp.exp2((masked - peak) * c2)
+        total = jnp.sum(expo, axis=0, keepdims=True)
+        mixed = lax.dot_general(
+            kv[r, 1], expo.astype(jnp.bfloat16), (((0,), (0,)), ((), ())),
+            preferred_element_type=jnp.float32)
+        if r == 0:
+            top, denom, numer = peak, total, mixed
+        else:
+            before = run[u, 0:1]
+            top = jnp.maximum(before, peak)
+            keep, add = jnp.exp2((before - top) * c2), jnp.exp2((peak - top) * c2)
+            denom = run[u, 1:2] * keep + total * add
+            numer = acc[u] * keep + mixed * add
+        if r < GANG - 1:
+            run[u, 0:1], run[u, 1:2] = top, denom
+            acc[u] = numer
+        else:
+            most = jnp.maximum(jnp.max(jnp.abs(numer), axis=0, keepdims=True), TINY)
+            level = jnp.round(numer * (STEPS / most))
+            rows = level.T.astype(jnp.int32).astype(jnp.int16).reshape(group, T, R, hd)
+            for k in range(group):
+                j = u * group + k
+                osend[j] = rows[k]
+                stats = [x[:, k * B:(k + 1) * B] for x in (top, denom, most)]
+                ssend[j] = jnp.concatenate(stats + stats[:1] * 5, axis=0)
+                for i in range(T):
+                    if j or i:
+                        s_copy(j, i).start()
+                        o_copy(j, i).start()
     orecv[0, me] = osend[0, me]
     srecv[0, me] = ssend[0]
     for j in range(H):
@@ -211,7 +213,15 @@
         first = g * heads * hd
         out_ref[:, first:first + heads * hd] = jnp.concatenate(
             [final[h * tokens:(h + 1) * tokens] for h in range(heads)], axis=1).astype(out_ref.dtype)
-    lse_ref[...] = lsebuf[me]
+    spot = lax.broadcasted_iota(jnp.int32, (heads, B), 1)
+    row = lax.broadcasted_iota(jnp.int32, (heads, B), 0)
+    spread = jnp.where(lax.div(lax.rem(spot, jnp.int32(R)), jnp.int32(tokens)) == row, lsebuf[me, 0:1], 0.0)
+    spot = lax.broadcasted_iota(jnp.int32, (block, B), 1)
+    row = lax.broadcasted_iota(jnp.int32, (block, B), 0)
+    pick = lax.div(spot, jnp.int32(R)) * tokens + lax.rem(spot, jnp.int32(tokens)) == row
+    lse_ref[...] = lax.dot_general(
+        spread, pick.astype(jnp.float32), (((1,), (1,)), ((), ())),
+        precision=lax.Precision.HIGHEST, preferred_element_type=jnp.float32)
     for j in range(H):
         for i in range(T):
             if j or i:
@@ -220,6 +230,17 @@
                 o_copy(j, i).wait_send()
     for copy in far + near + relay:
         copy.wait_send()
+
+
+def hand_over(out_ref, lse_ref, out_to, lse_to, sems):
+    copies = [
+        pltpu.make_async_copy(out_ref, out_to, sems.at[0]),
+        pltpu.make_async_copy(lse_ref, lse_to, sems.at[1]),
+    ]
+    for copy in copies:
+        copy.start()
+    for copy in copies:
+        copy.wait()
 
 
 def shards(q_new, kv_new, kv_cache, cache_lens, segment_ids):
@@ -241,7 +262,7 @@
         functools.partial(kernel, H, T, R, hd ** -0.5),
         out_shape=(
             jax.ShapeDtypeStruct(q_new.shape, jnp.bfloat16),
-            jax.ShapeDtypeStruct((8, B), jnp.float32),
+            jax.ShapeDtypeStruct((heads, block), jnp.float32),
         ),
         in_specs=[hbm] * 5,
         out_specs=(vmem, vmem),
@@ -265,10 +286,17 @@
             dma((H, T)), dma((H, T)), dma((GANG, 2)), dma((GANG, 2)), dma((5,)), dma((H, T)), dma((H, T)), dma((H, T)), dma((H, T)),
         ],
         compiler_params=pltpu.CompilerParams(
-            collective_id=0, has_side_effects=True, vmem_limit_bytes=48 * 2 ** 20),
+            collective_id=0, has_side_effects=True, vmem_limit_bytes=60 * 2 ** 20),
     )(q_new, kv_cache, kv_new, cache_lens, segment_ids.reshape(1, new))
-    lse = lse[0].reshape(T, heads, tokens).transpose(0, 2, 1).reshape(block, heads)
-    return out, lse
+    out, lse = pl.pallas_call(
+        hand_over,
+        out_shape=(jax.ShapeDtypeStruct(out.shape, out.dtype), jax.ShapeDtypeStruct(lse.shape, lse.dtype)),
+        in_specs=[hbm] * 2,
+        out_specs=(hbm, hbm),
+        scratch_shapes=[dma((2,))],
+        compiler_params=pltpu.CompilerParams(vmem_limit_bytes=60 * 2 ** 20),
+    )(out, lse)
+    return out, lse.T
 
 
 def solution(mesh):

time: 26.7 us -> 25.2 us (0.944)
  local copies, waits for them, and re-layouts: 4.46 us -> 0 us
  Pallas kernels: 21.3 us -> 24.4 us
    unnamed x11 -> x0, local copies, waits for them, and re-layouts: 3.68 us -> none
    pallas_call x0 -> x1, Pallas kernels: none -> 2.24 us  [shards(): pl.pallas_call(hand_over, out_shape=(jax.ShapeDtypeStruct(out.shape, out....]
    pallas_call x1, Pallas kernels: 21.3 us -> 22.2 us  [shards(): pl.pallas_call(functools.partial(kernel, H, T, R, hd ** (-0.5)), out_shap...]
    reshape x1 -> x0, local copies, waits for them, and re-layouts: 0.67 us -> none  [shards(): lse[0].reshape(T, heads, tokens).transpose(0, 2, 1).reshape(block, heads)]
where the time goes in v3:
time: 25.2 us; the launch traced here: 25.1 us
  Pallas kernels  24.4 us (97%)
  between operations  0.64 us (3%)
    pallas_call x1, Pallas kernels, shards(): pl.pallas_call(functools.partial(kernel, H, T, R, hd ** (-0.5)), out_shap...  22.2 us
    pallas_call x1, Pallas kernels, shards(): pl.pallas_call(hand_over, out_shape=(jax.ShapeDtypeStruct(out.shape, out....  2.24 us

profile of v3, /device:TPU:0, one launch (start us, length us, event | category | flops | bytes accessed | tf_op | source)
XLA Modules:
  0.0 25.1 jit_solution(14291749049458834625)
XLA Ops:
  0.6 22.2 %shard_map.68 = (bf16[8,2048]{1,0:T(8,128)(2,1)}, f32[8,16]{1,0:T(8,128)}) custom-call(bf16[8,2048]{1,0:T(8,128)(2,1)} %q_hbm.1, bf16[2,496,128]{2,1,0:T(8,128)(2,1)} %cache_ref.1, bf16[2,16,128]{2,1,0:T(8,128)(2,1)} %new_ref.1, s32[16]{0:T(128)} %lens_hbm.1, s32[1,256]{1,0:T(1,128)} %bitcast.2), custom_call_target="tpu_custom_call" | custom-call | tf_op jit(solution)/shard_map/pallas_call | solution.py:261
  22.8 2.2 %shard_map.69 = (bf16[8,2048]{1,0:T(8,128)(2,1)}, f32[8,16]{1,0:T(8,128)}) custom-call(bf16[8,2048]{1,0:T(8,128)(2,1)} %get-tuple-element.6.out_ref, f32[8,16]{1,0:T(8,128)} %get-tuple-element.7.lse_ref), custom_call_target="tpu_custom_call" | custom-call | tf_op jit(solution)/shard_map/pallas_call | solution.py:291

commit v4 on v3

--- a/solution.py
+++ b/solution.py
@@ -232,15 +232,9 @@
         copy.wait_send()
 
 
-def hand_over(out_ref, lse_ref, out_to, lse_to, sems):
-    copies = [
-        pltpu.make_async_copy(out_ref, out_to, sems.at[0]),
-        pltpu.make_async_copy(lse_ref, lse_to, sems.at[1]),
-    ]
-    for copy in copies:
-        copy.start()
-    for copy in copies:
-        copy.wait()
+def hand_over(out_ref, lse_ref, out_to, lse_to):
+    out_to[...] = out_ref[...]
+    lse_to[...] = lse_ref[...]
 
 
 def shards(q_new, kv_new, kv_cache, cache_lens, segment_ids):
@@ -291,9 +285,8 @@
     out, lse = pl.pallas_call(
         hand_over,
         out_shape=(jax.ShapeDtypeStruct(out.shape, out.dtype), jax.ShapeDtypeStruct(lse.shape, lse.dtype)),
-        in_specs=[hbm] * 2,
-        out_specs=(hbm, hbm),
-        scratch_shapes=[dma((2,))],
+        in_specs=[vmem] * 2,
+        out_specs=(vmem, vmem),
         compiler_params=pltpu.CompilerParams(vmem_limit_bytes=60 * 2 ** 20),
     )(out, lse)
     return out, lse.T

time: 25.2 us -> 24.4 us (0.968)
  Pallas kernels: 24.4 us -> 23.6 us
    pallas_call x1, Pallas kernels: 2.24 us -> 1.38 us  [shards(): pl.pallas_call(hand_over, out_shape=(jax.ShapeDtypeStruct(out.shape, out....]
where the time goes in v4:
time: 24.4 us; the launch traced here: 24.2 us
  Pallas kernels  23.6 us (97%)
  between operations  0.64 us (3%)
    pallas_call x1, Pallas kernels, shards(): pl.pallas_call(functools.partial(kernel, H, T, R, hd ** (-0.5)), out_shap...  22.2 us
    pallas_call x1, Pallas kernels, shards(): pl.pallas_call(hand_over, out_shape=(jax.ShapeDtypeStruct(out.shape, out....  1.38 us

profile of v4, /device:TPU:0, one launch (start us, length us, event | category | flops | bytes accessed | tf_op | source)
XLA Modules:
  0.0 24.2 jit_solution(2278136445288728154)
XLA Ops:
  0.6 22.2 %shard_map.68 = (bf16[8,2048]{1,0:T(8,128)(2,1)}, f32[8,16]{1,0:T(8,128)}) custom-call(bf16[8,2048]{1,0:T(8,128)(2,1)} %q_hbm.1, bf16[2,496,128]{2,1,0:T(8,128)(2,1)} %cache_ref.1, bf16[2,16,128]{2,1,0:T(8,128)(2,1)} %new_ref.1, s32[16]{0:T(128)} %lens_hbm.1, s32[1,256]{1,0:T(1,128)} %bitcast.2), custom_call_target="tpu_custom_call" | custom-call | tf_op jit(solution)/shard_map/pallas_call | solution.py:255
  22.8 1.4 %shard_map.69 = (bf16[8,2048]{1,0:T(8,128)(2,1)}, f32[8,16]{1,0:T(8,128)}) custom-call(bf16[8,2048]{1,0:T(8,128)(2,1)} %get-tuple-element.6.out_ref, f32[8,16]{1,0:T(8,128)} %get-tuple-element.7.lse_ref), custom_call_target="tpu_custom_call" | custom-call | tf_op jit(solution)/shard_map/pallas_call | solution.py:285
